TPU v7x, 128 devices: a whole 4x4x4 slice. The times are simulated.
128 devices in a mesh: blk: 32 (over y, z_hi, x), dp: 4 (over z_lo, core).
Axes of the slice: x: 4, y: 4, z: 4 (z_hi: 2, z_lo: 2; z = z_hi * 2 + z_lo), core: 2. Of those that a mesh axis runs over, the one named last changes fastest.
Arguments:
- image_embed: bfloat16 [98304, 1152], P(('dp', 'blk')), parts along dimension 0, may hold values from -0.1875 to 0.1875
- text_embed: bfloat16 [98304, 1152], P(('dp', 'blk')), parts along dimension 0, may hold values from -0.1875 to 0.1875
- logit_scale: float32 [1], replicated, may hold values from 4 to 10
- logit_bias: float32 [1], replicated, may hold values from -4 to -1
Outputs:
- image_grad: float32 [98304, 1152], P(('dp', 'blk')), parts along dimension 0
- text_grad: float32 [98304, 1152], P(('dp', 'blk')), parts along dimension 0
There are 4 independent parts, one for each index of `dp`. A program takes and returns all parts, laid end to end along the dimension named above; an argument that names none is the same for every part. Nothing has to cross between parts.
All inputs are finite; a program needn't handle non-finite values.
Results may differ from a plain program's by a relative error of at most 0.0045.
Values may be sent and summed in bfloat16 or wider, within the bound.
A program may use at most 64 MiB of HBM per device.

v0:
```python
import jax
import jax.numpy as jnp
from jax import lax
from jax.sharding import PartitionSpec as P

ROUNDS = 4


epsilon = 1e-06


def passed_along(value, axis, steps):
    count = lax.axis_size(axis)
    pairs = [(source, (source + steps) % count) for source in range(count)]
    return lax.ppermute(value, axis, pairs)


def normalize(raw):
    values = raw.astype(jnp.float32)
    inverse = lax.rsqrt(jnp.sum(values * values, axis=1, keepdims=True) + epsilon)
    return (values * inverse, inverse)


def pair_weights(image_low, text_low, temper, offset, positive):
    logits = (
        temper
        * lax.dot_general(
            image_low, text_low, (((1,), (1,)), ((), ())), preferred_element_type=jnp.float32
        )
        + offset
    )
    return (temper * (jax.nn.sigmoid(logits) - positive)).astype(jnp.bfloat16)


def image_side(weights, text_low):
    return jnp.dot(weights, text_low, preferred_element_type=jnp.float32)


def text_side(weights, image_low):
    return lax.dot_general(
        weights, image_low, (((0,), (0,)), ((), ())), preferred_element_type=jnp.float32
    )


def project_back(unit, inverse, grad_unit):
    return (grad_unit - unit * jnp.sum(unit * grad_unit, axis=1, keepdims=True)) * inverse


def shards(image_embed, text_embed, logit_scale, logit_bias):
    temper = logit_scale[0]
    offset = logit_bias[0]
    row_count = image_embed.shape[0]
    unit_image, inv_image = normalize(image_embed)
    unit_text, inv_text = normalize(text_embed)
    image_low = unit_image.astype(jnp.bfloat16)
    own_text = unit_text.astype(jnp.bfloat16)
    current = own_text
    image_sums = jnp.zeros(image_embed.shape, jnp.float32)
    running = jnp.zeros(text_embed.shape, jnp.float32)
    for round_index in range(ROUNDS):
        if round_index > 0:
            current = passed_along(current, "blk", 1)
        if round_index == 0:
            positive = jnp.eye(row_count, dtype=jnp.float32)
        else:
            positive = jnp.zeros((row_count, row_count), jnp.float32)
        weights = pair_weights(image_low, current, temper, offset, positive)
        image_sums = image_sums + image_side(weights, current)
        text_term = text_side(weights, image_low)
        if round_index == 0:
            running = text_term
        else:
            running = passed_along(running, "blk", 1) + text_term
    running = passed_along(running, "blk", 1 - ROUNDS)
    image_grad = project_back(unit_image, inv_image, image_sums)
    text_grad = project_back(unit_text, inv_text, running)
    return (image_grad, text_grad)


def solution(mesh):
    return jax.shard_map(
        shards,
        mesh=mesh,
        in_specs=(P(("dp", "blk"), None), P(("dp", "blk"), None), P(), P()),
        out_specs=(P(("dp", "blk"), None), P(("dp", "blk"), None)),
        check_vma=False,
    )
```

profile of v0, /device:TPU:1, one launch (start us, length us, event | category | flops | bytes accessed | tf_op | source)
XLA Modules:
  0.0 464.1 jit_solution(12886434651205312222)
XLA Ops:
  0.6 0.0 copy-start
  0.6 2.0 fusion.9
  2.7 0.0 copy-done
  2.7 0.0 copy-start.1
  2.7 0.4 fusion.13
  3.1 0.4 fusion.2
  4.8 0.0 copy-done.1
  4.8 2.0 multiply_convert_fusion.3
  6.8 1.9 fusion.19
  8.7 2.1 collective-permute-start.3
  10.8 1.2 collective-permute-start
  12.0 120.0 %collective-permute-done = bf16[768,1152]{1,0:T(8,128)(2,1)S(1)} collective-permute-done((bf16[768,1152]{1,0:T(8,128)(2,1)S(1)}, bf16[768,1152]{1,0:T(8,128)(2,1)S(1)}, u32[]{:S(2)}, u32[]{:S(2)}) %collective-permute-start) | collective-permute-done | bytes 1769504 | tf_op jit(solution)/shard_map/ppermute | solution.py:15
  132.0 2.0 multiply_convert_fusion.2
  134.0 0.0 collective-permute-done.3
  134.0 1.9 convolution_add_fusion
  136.0 0.1 collective-permute-start.4
  136.0 0.3 collective-permute-start.1
  136.3 120.2 %collective-permute-done.1 = bf16[768,1152]{1,0:T(8,128)(2,1)S(1)} collective-permute-done((bf16[768,1152]{1,0:T(8,128)(2,1)S(1)}, bf16[768,1152]{1,0:T(8,128)(2,1)S(1)}, u32[]{:S(2)}, u32[]{:S(2)}) %collective-permute-start.1) | collective-permute-done | bytes 1769504 | tf_op jit(solution)/shard_map/ppermute | solution.py:15
  256.5 2.0 multiply_convert_fusion.1
  258.5 1.9 fusion.16
  260.3 0.0 collective-permute-done.4
  260.4 0.4 add.79
  260.7 0.1 collective-permute-start.5
  260.8 0.1 collective-permute-start.2
  260.9 119.4 %collective-permute-done.2 = bf16[768,1152]{1,0:T(8,128)(2,1)S(1)} collective-permute-done((bf16[768,1152]{1,0:T(8,128)(2,1)S(1)}, bf16[768,1152]{1,0:T(8,128)(2,1)S(1)}, u32[]{:S(2)}, u32[]{:S(2)}) %collective-permute-start.2) | collective-permute-done | bytes 1769504 | tf_op jit(solution)/shard_map/ppermute | solution.py:15
  380.3 2.0 multiply_convert_fusion
  382.3 1.8 fusion.14
  384.2 0.0 collective-permute-done.5
  384.2 0.4 add.80
  384.5 0.3 collective-permute-start.6
  384.8 1.7 fusion.25
  386.6 1.8 convolution_add_fusion.3
  388.3 1.8 convolution_add_fusion.2
  390.1 2.0 fusion.6
  392.1 2.5 fusion.8
  394.6 66.4 %collective-permute-done.6 = f32[768,1152]{1,0:T(8,128)S(1)} collective-permute-done((f32[768,1152]{1,0:T(8,128)S(1)}, f32[768,1152]{1,0:T(8,128)S(1)}, u32[]{:S(2)}, u32[]{:S(2)}) %collective-permute-start.6) | collective-permute-done | bytes 3538976 | tf_op jit(solution)/shard_map/ppermute | solution.py:15
  461.0 0.6 fusion.10
  461.6 2.5 fusion.12
  (2 shorter events, 0.0 us)
Async XLA Ops:
  0.6 2.0 copy-start
  2.7 2.1 copy-start.1
  8.7 125.3 %collective-permute-start.3 = (f32[768,1152]{1,0:T(8,128)S(1)}, f32[768,1152]{1,0:T(8,128)S(1)}, u32[]{:S(2)}, u32[]{:S(2)}) collective-permute-start(f32[768,1152]{1,0:T(8,128)S(1)} %fusion.19), channel_id=1, source_target_pairs={{0,4},{4,8},{8,12},{12,16},{16,20},{20,24},{24,28},{28,32},{32,36}... | collective-permute-start | bytes 10616840 | tf_op jit(solution)/shard_map/ppermute | solution.py:15
  10.8 121.2 %collective-permute-start = (bf16[768,1152]{1,0:T(8,128)(2,1)S(1)}, bf16[768,1152]{1,0:T(8,128)(2,1)S(1)}, u32[]{:S(2)}, u32[]{:S(2)}) collective-permute-start(bf16[768,1152]{1,0:T(8,128)(2,1)S(1)} %fusion.2), channel_id=1, source_target_pairs={{0,4},{4,8},{8,12},{12,16},{16,20},{20,24},{24,28},{28,32},{32,36}... | collective-permute-start | bytes 5308424 | tf_op jit(solution)/shard_map/ppermute | solution.py:15
  136.0 124.4 %collective-permute-start.4 = (f32[768,1152]{1,0:T(8,128)S(1)}, f32[768,1152]{1,0:T(8,128)S(1)}, u32[]{:S(2)}, u32[]{:S(2)}) collective-permute-start(f32[768,1152]{1,0:T(8,128)S(1)} %convolution_add_fusion), channel_id=1, source_target_pairs={{0,4},{4,8},{8,12},{12,16},{16,20},{20,24},{24,28},{28,32},{32,36}... | collective-permute-start | bytes 10616840 | tf_op jit(solution)/shard_map/ppermute | solution.py:15
  136.0 120.4 %collective-permute-start.1 = (bf16[768,1152]{1,0:T(8,128)(2,1)S(1)}, bf16[768,1152]{1,0:T(8,128)(2,1)S(1)}, u32[]{:S(2)}, u32[]{:S(2)}) collective-permute-start(bf16[768,1152]{1,0:T(8,128)(2,1)S(1)} %collective-permute-done), channel_id=1, source_target_pairs={{0,4},{4,8},{8,12},{12,16},{16,20},{20,24},{24,28},{28,32},{32,36}... | collective-permute-start | bytes 5308424 | tf_op jit(solution)/shard_map/ppermute | solution.py:15
  260.7 123.4 %collective-permute-start.5 = (f32[768,1152]{1,0:T(8,128)S(1)}, f32[768,1152]{1,0:T(8,128)S(1)}, u32[]{:S(2)}, u32[]{:S(2)}) collective-permute-start(f32[768,1152]{1,0:T(8,128)S(1)} %add.79), channel_id=1, source_target_pairs={{0,4},{4,8},{8,12},{12,16},{16,20},{20,24},{24,28},{28,32},{32,36}... | collective-permute-start | bytes 10616840 | tf_op jit(solution)/shard_map/ppermute | solution.py:15
  260.8 119.5 %collective-permute-start.2 = (bf16[768,1152]{1,0:T(8,128)(2,1)S(1)}, bf16[768,1152]{1,0:T(8,128)(2,1)S(1)}, u32[]{:S(2)}, u32[]{:S(2)}) collective-permute-start(bf16[768,1152]{1,0:T(8,128)(2,1)S(1)} %collective-permute-done.1), channel_id=1, source_target_pairs={{0,4},{4,8},{8,12},{12,16},{16,20},{20,24},{24,28},{28,32},{32,36}... | collective-permute-start | bytes 5308424 | tf_op jit(solution)/shard_map/ppermute | solution.py:15
  384.5 76.5 %collective-permute-start.6 = (f32[768,1152]{1,0:T(8,128)S(1)}, f32[768,1152]{1,0:T(8,128)S(1)}, u32[]{:S(2)}, u32[]{:S(2)}) collective-permute-start(f32[768,1152]{1,0:T(8,128)S(1)} %add.80), channel_id=1, source_target_pairs={{0,116},{4,120},{8,124},{12,0},{16,4},{20,8},{24,12},{28,16},{32,2... | collective-permute-start | bytes 10616840 | tf_op jit(solution)/shard_map/ppermute | solution.py:15
where the time goes:
time: 467 us; the launch traced here: 464 us
  waiting for transfers between devices  426 us (91%)
  matrix products  22.8 us (5%)
  other arithmetic  9.05 us (2%)
    ppermute x7, waiting for transfers between devices, passed_along(): return lax.ppermute(value, axis, pairs)  426 us
  transfers between devices with their start and end apart: 7, of which 4 were waited for; matrix products, arithmetic and copies ran while one was open for 4% of the time, Pallas kernels for 0%

commit v1 on v0

v1 whole, which is shorter than its diff:
```python
import functools

import jax
import jax.numpy as jnp
from jax import lax
from jax.experimental import pallas as pl
from jax.experimental.pallas import tpu as pltpu
from jax.sharding import PartitionSpec as P

MESH = pl.DeviceIdType.MESH
ROW = 4
PARTS = 3
BACK = 6

epsilon = 1e-06

OWN_A, OWN_B, LENT_A, LENT_B, FAR_B = range(5)

def tile_order():
    steps = []

    def add(a, i, b, t, await_=-1, done=0, piece=0):
        steps.append((a, i, b, t, await_, done, piece))

    for i in range(PARTS):
        for t in range(PARTS):
            add(OWN_A, i, OWN_B, t)
    for c in range(PARTS - 1):
        add(OWN_A, 0, LENT_B, c, await_=c)
        for i in range(1, PARTS):
            add(OWN_A, i, LENT_B, c)
        for b in (LENT_B, -1):
            for k in range(c):
                add(LENT_A, k, b, c)
            for k in range(c + 1):
                add(LENT_A, c, b, k)
    c = PARTS - 1
    first = True
    for k in range(c):
        add(LENT_A, c, LENT_B, k, await_=c if first else -1, done=1, piece=k)
        first = False
        add(LENT_A, k, LENT_B, c)
        add(LENT_A, k, -1, c, done=2, piece=k)
    for k in range(c):
        add(LENT_A, c, -1, k, done=4, piece=k)
    for i in range(PARTS):
        add(OWN_A, i, LENT_B, c)
    add(LENT_A, c, LENT_B, c, done=1, piece=c)
    add(LENT_A, c, -1, c, done=6, piece=c)
    return steps


def pick(step, values):
    total = jnp.int32(0)
    for k, v in enumerate(values):
        if v != 0:
            total = total + jnp.where(step == k, jnp.int32(v), jnp.int32(0))
    return total


def kernel(
    image_ref, text_ref, scale_ref, bias_ref, image_out, text_out,
    raw, inv, low, acc, give, got,
    load_sem, send_sem, recv_sem, back_send_sem, back_recv_sem, out_sem,
):
    rows, _ = image_ref.shape
    size = rows // PARTS
    back = rows // BACK
    blk = lax.axis_index("blk")
    core = lax.rem(lax.axis_index("dp"), 2)
    x = lax.rem(blk, ROW)
    line = lax.div(blk, ROW)
    n_lines = lax.axis_size("blk") // ROW
    place = x + core * (ROW - 1 - 2 * x)
    sign = 1 - 2 * core
    odd = lax.rem(place, 2)
    upper = lax.div(place, 2)

    def block_at(shift, column):
        return lax.rem(line + shift + n_lines, n_lines) * ROW + column

    peer = block_at(0, x + 1 - 2 * lax.rem(x, 2))
    lent_to = block_at(sign * upper, ROW - 1 - x)
    lent_by = block_at(sign * (upper - 1), ROW - 1 - x)
    far_to = block_at(sign, x)
    far_by = block_at(-sign, x)

    def on(block):
        return {"blk": block}

    barrier = pltpu.get_barrier_semaphore()
    for block in (peer, lent_to, lent_by):
        pl.semaphore_signal(barrier, inc=1, device_id=on(block), device_id_type=MESH)

    @pl.when(odd == 1)
    def _():
        for block in (far_to, far_by):
            pl.semaphore_signal(barrier, inc=1, device_id=on(block), device_id_type=MESH)

    def load(source, slot, c):
        part = pl.ds(c * size, size)
        return pltpu.make_async_copy(
            source.at[part], raw.at[slot, part], load_sem.at[slot, c]
        )

    for c in range(PARTS):
        load(image_ref, core, c).start()
        load(text_ref, 1 - core, c).start()

    def send(flow, c):
        part = pl.ds(c * size, size)
        slot, place_, block = (
            (OWN_A, LENT_A, peer),
            (OWN_B, LENT_B, lent_to),
            (OWN_B, FAR_B, far_to),
        )[flow]
        return pltpu.make_async_remote_copy(
            low.at[slot, part], low.at[place_, part],
            send_sem.at[flow, c], recv_sem.at[flow, c],
            device_id=on(block), device_id_type=MESH,
        )

    def give_back(flow, r):
        part = pl.ds(r * back, back)
        block = (peer, lent_by, far_by)[flow]
        return pltpu.make_async_remote_copy(
            give.at[flow, part], got.at[flow, part],
            back_send_sem.at[flow, r], back_recv_sem.at[flow, r],
            device_id=on(block), device_id_type=MESH,
        )

    for c in range(PARTS):
        load(image_ref, core, c).wait()
        load(text_ref, 1 - core, c).wait()

        def normalize(k, _):
            slot = lax.div(k, 4)
            part = pl.ds(c * size + lax.rem(k, 4) * (size // 4), size // 4)
            values = raw[slot, part].astype(jnp.float32)
            inverse = lax.rsqrt(jnp.sum(values * values, axis=1, keepdims=True) + epsilon)
            inv[slot, part] = inverse
            low[slot, part] = (values * inverse).astype(jnp.bfloat16)
            return 0

        lax.fori_loop(0, 8, normalize, 0)
        if c == 0:
            pl.semaphore_wait(barrier, 3 + 2 * odd)

        send(0, c).start()
        send(1, c).start()

        @pl.when(odd == 1)
        def _():
            send(2, c).start()

    def clear(k, _):
        part = pl.ds(k * 64, 64)
        for slot in range(5):
            acc[slot, part] = jnp.zeros((64, acc.shape[2]), jnp.float32)
        return 0

    lax.fori_loop(0, rows // 64, clear, 0)

    temper = scale_ref[0]
    offset = bias_ref[0]
    order = tile_order()
    columns = list(zip(*order))

    def flush(flow, slot, piece):
        for h in range(BACK // PARTS):
            r = piece * (BACK // PARTS) + h
            part = pl.ds(r * back, back)
            give[flow, part] = acc[slot, part].astype(jnp.bfloat16)
            give_back(flow, r).start()

    def tile(step, _):
        a = pick(step, columns[0])
        i = pick(step, columns[1]) * size
        b = pick(step, [v if v >= 0 else 0 for v in columns[2]])
        b = b + pick(step, [int(v < 0) for v in columns[2]]) * (OWN_B + (FAR_B - OWN_B) * odd)
        t = pick(step, columns[3]) * size
        awaited = pick(step, [v + 1 for v in columns[4]])
        done = pick(step, columns[5])
        piece = pick(step, columns[6])

        @pl.when(awaited > 0)
        def _():
            send(0, awaited - 1).wait_recv()
            send(1, awaited - 1).wait_recv()

            @pl.when(odd == 1)
            def _():
                send(2, awaited - 1).wait_recv()

        part_a = pl.ds(pl.multiple_of(i, size), size)
        part_b = pl.ds(pl.multiple_of(t, size), size)
        first = low[a, part_a]
        second = low[b, part_b]
        logits = lax.dot_general(
            first, second, (((1,), (1,)), ((), ())), preferred_element_type=jnp.float32
        )
        row = lax.broadcasted_iota(jnp.int32, (size, size), 0)
        column = lax.broadcasted_iota(jnp.int32, (size, size), 1)
        own = jnp.logical_and(a == OWN_A, jnp.logical_and(b == OWN_B, i == t))
        span = jnp.where(own, 0, 2 * size)
        positive = jnp.where(row - column == span, 1.0, 0.0)
        weights = (temper * (jax.nn.sigmoid(temper * logits + offset) - positive)).astype(
            jnp.bfloat16
        )
        acc[a, part_a] += jnp.dot(weights, second, preferred_element_type=jnp.float32)
        acc[b, part_b] += lax.dot_general(
            weights, first, (((0,), (0,)), ((), ())), preferred_element_type=jnp.float32
        )

        @pl.when(lax.rem(done, 2) == 1)
        def _():
            flush(1, LENT_B, piece)

        @pl.when(lax.rem(lax.div(done, 2), 2) == 1)
        def _():
            flush(0, LENT_A, piece)

        @pl.when(jnp.logical_and(done >= 4, odd == 1))
        def _():
            flush(2, FAR_B, piece)

        return 0

    lax.fori_loop(0, len(order), tile, 0)

    def finish(r, _):
        part = pl.ds(pl.multiple_of(r * back, back), back)
        give_back(0, r).wait_recv()
        give_back(1, r).wait_recv()
        acc[OWN_A, part] += got[0, part].astype(jnp.float32)
        acc[OWN_B, part] += got[1, part].astype(jnp.float32)

        @pl.when(odd == 1)
        def _():
            give_back(2, r).wait_recv()
            acc[OWN_B, part] += got[2, part].astype(jnp.float32)

        for slot in (0, 1):
            inverse = inv[slot, part]
            unit = raw[slot, part].astype(jnp.float32) * inverse
            grad = acc[slot, part]
            acc[slot, part] = (
                grad - unit * jnp.sum(unit * grad, axis=1, keepdims=True)
            ) * inverse
        store(image_out, core, r).start()
        store(text_out, 1 - core, r).start()
        return 0

    def store(target, slot, r):
        part = pl.ds(pl.multiple_of(r * back, back), back)
        return pltpu.make_async_copy(acc.at[slot, part], target.at[part], out_sem.at[slot, r])

    lax.fori_loop(0, BACK, finish, 0)

    for flow in range(3):
        def settle(flow=flow):
            for c in range(PARTS):
                send(flow, c).wait_send()
            for r in range(BACK):
                give_back(flow, r).wait_send()

        if flow < 2:
            settle()
        else:
            pl.when(odd == 1)(settle)
    for r in range(BACK):
        store(image_out, core, r).wait()
        store(text_out, 1 - core, r).wait()


def shards(image_embed, text_embed, logit_scale, logit_bias):
    rows, width = image_embed.shape
    stack = lambda n, kind: pltpu.VMEM((n, rows, width), kind)
    return pl.pallas_call(
        kernel,
        out_shape=[jax.ShapeDtypeStruct((rows, width), jnp.float32)] * 2,
        in_specs=[pl.BlockSpec(memory_space=pl.ANY)] * 2
        + [pl.BlockSpec(memory_space=pltpu.SMEM)] * 2,
        out_specs=[pl.BlockSpec(memory_space=pl.ANY)] * 2,
        scratch_shapes=[
            stack(2, jnp.bfloat16),
            pltpu.VMEM((2, rows, 1), jnp.float32),
            stack(5, jnp.bfloat16),
            stack(5, jnp.float32),
            stack(3, jnp.bfloat16),
            stack(3, jnp.bfloat16),
            pltpu.SemaphoreType.DMA((2, PARTS)),
            pltpu.SemaphoreType.DMA((3, PARTS)),
            pltpu.SemaphoreType.DMA((3, PARTS)),
            pltpu.SemaphoreType.DMA((3, BACK)),
            pltpu.SemaphoreType.DMA((3, BACK)),
            pltpu.SemaphoreType.DMA((2, BACK)),
        ],
        compiler_params=pltpu.CompilerParams(
            collective_id=0, has_side_effects=True, vmem_limit_bytes=60 * 1024 * 1024
        ),
        cost_estimate=pl.CostEstimate(
            flops=24 * rows * rows * width, bytes_accessed=12 * rows * width,
            transcendentals=4 * rows * rows,
        ),
        name="pair_gradients",
    )(image_embed, text_embed, logit_scale, logit_bias)


def solution(mesh):
    return jax.shard_map(
        shards,
        mesh=mesh,
        in_specs=(P(("dp", "blk"), None), P(("dp", "blk"), None), P(), P()),
        out_specs=(P(("dp", "blk"), None), P(("dp", "blk"), None)),
        check_vma=False,
    )
```

time: 467 us -> 107 us (0.23)
  waiting for transfers between devices: 426 us -> 0 us
  Pallas kernels: 0 us -> 98.6 us
  matrix products: 22.8 us -> 0 us
  other arithmetic: 9.05 us -> 0 us
  local copies, waits for them, and re-layouts: 0.01 us -> 5.97 us
    ppermute x7 -> x0, waiting for transfers between devices: 426 us -> none  [passed_along(): return lax.ppermute(value, axis, pairs)]
    pallas_call x0 -> x1, Pallas kernels: none -> 98.6 us  [shards(): pl.pallas_call(kernel, out_shape=[jax.ShapeDtypeStruct((rows, width), jnp...]
    dot_general x12 -> x0, matrix products: 22.8 us -> none  [the longest x4 7.99 us: pair_weights(): lax.dot_general(image_low, text_low, (((1,), (1,)), ((), ())), preferred_...]
    unnamed x4, local copies, waits for them, and re-layouts: 0.01 us -> 5.97 us
    mul x2 -> x0, other arithmetic: 4.92 us -> none  [project_back(): (grad_unit - unit * jnp.sum(unit * grad_unit, axis=1, keepdims=True)) * i...]
  transfers between devices with their start and end apart: 7 -> 0, of which waited for: 4 -> 0; matrix products, arithmetic and copies ran while one was open for 4% -> 0% of each run, Pallas kernels for 0% -> 0%
where the time goes in v1:
time: 107 us; the launch traced here: 106 us
  Pallas kernels  98.6 us (92%)
  local copies, waits for them, and re-layouts  5.97 us (6%)
  between operations  1.94 us (2%)
    pallas_call x1, Pallas kernels, shards(): pl.pallas_call(kernel, out_shape=[jax.ShapeDtypeStruct((rows, width), jnp...  98.6 us
    unnamed x4, local copies, waits for them, and re-layouts  5.97 us

profile of v1, /device:TPU:1, one launch (start us, length us, event | category | flops | bytes accessed | tf_op | source)
XLA Modules:
  0.0 106.5 jit_solution(8002446312597736892)
XLA Ops:
  1.9 98.6 %pair_gradients.1 = (f32[768,1152]{1,0:T(8,128)}, f32[768,1152]{1,0:T(8,128)}) custom-call(bf16[768,1152]{1,0:T(8,128)(2,1)} %image_ref.1, bf16[768,1152]{1,0:T(8,128)(2,1)} %text_ref.1, f32[1]{0:T(128)S(6)} %copy.8.scale_ref, f32[1]{0:T(128)S(6)} %copy.9.bias_ref), custom_call_target="tpu_custom_call" | custom-call | flops 16307453952 | bytes 10616832 | tf_op jit(solution)/shard_map/pair_gradients/pallas_call | solution.py:279
  100.5 0.0 copy-start
  100.5 4.2 %copy.10 = f32[768,1152]{1,0:T(8,128)} copy(f32[768,1152]{1,0:T(8,128)} %get-tuple-element.4) | data formatting | bytes 7077888
  104.7 0.0 copy-done
  104.7 1.8 %copy.11 = f32[768,1152]{1,0:T(8,128)} copy(f32[768,1152]{1,0:T(8,128)S(1)} %copy-done) | data formatting | bytes 7077888
Async XLA Ops:
  100.5 4.2 %copy-start = (f32[768,1152]{1,0:T(8,128)S(1)}, f32[768,1152]{1,0:T(8,128)}, u32[]{:S(2)}) copy-start(f32[768,1152]{1,0:T(8,128)} %get-tuple-element.5) | copy-start | bytes 10616836

commit v2 on v1

v2 whole, which is shorter than its diff:
```python
import functools

import jax
import jax.numpy as jnp
from jax import lax
from jax.experimental import pallas as pl
from jax.experimental.pallas import tpu as pltpu
from jax.sharding import PartitionSpec as P

MESH = pl.DeviceIdType.MESH
ROW = 4
CUTS = ((0, 512), (512, 256))
PARTS = len(CUTS)
STEP = 256
BACK = 6

epsilon = 1e-06

LOWER = ([(0, 0), (2, 0), (0, 1)], [(1, 0), (2, 1)], [(1, 1)])
UPPER = ([(1, 0), (1, 1)], [(0, 0), (2, 0)], [(0, 1), (2, 1)])


def kernel(
    image_ref, text_ref, scale_ref, bias_ref, out,
    raw, inv, firsts, seconds, weights, give, got,
    load_sem, send_sem, recv_sem, back_send_sem, back_recv_sem,
):
    rows, _ = image_ref.shape
    back = rows // BACK
    blk = lax.axis_index("blk")
    core = lax.rem(lax.axis_index("dp"), 2)
    x = lax.rem(blk, ROW)
    line = lax.div(blk, ROW)
    n_lines = lax.axis_size("blk") // ROW
    place = x + core * (ROW - 1 - 2 * x)
    sign = 1 - 2 * core
    odd = lax.rem(place, 2)
    upper = lax.div(place, 2)

    def block_at(shift, column):
        return lax.rem(line + shift + n_lines, n_lines) * ROW + column

    peer = block_at(0, x + 1 - 2 * lax.rem(x, 2))
    lent_to = block_at(sign * upper, ROW - 1 - x)
    lent_by = block_at(sign * (upper - 1), ROW - 1 - x)
    far_to = block_at(sign, x)
    far_by = block_at(-sign, x)

    def on(block):
        return {"blk": block}

    barrier = pltpu.get_barrier_semaphore()
    for block in (peer, lent_to, lent_by):
        pl.semaphore_signal(barrier, inc=1, device_id=on(block), device_id_type=MESH)

    @pl.when(odd == 1)
    def _():
        for block in (far_to, far_by):
            pl.semaphore_signal(barrier, inc=1, device_id=on(block), device_id_type=MESH)

    def load(source, slot, c):
        part = pl.ds(*CUTS[c])
        return pltpu.make_async_copy(
            source.at[part], raw.at[slot, part], load_sem.at[slot, c]
        )

    for c in range(PARTS):
        load(image_ref, core, c).start()
        load(text_ref, 1 - core, c).start()

    def send(flow, c):
        start, count = CUTS[c]
        buffer, place_, block = (
            (firsts, 1, peer), (seconds, 1, lent_to), (seconds, 2, far_to)
        )[flow]
        return pltpu.make_async_remote_copy(
            buffer.at[pl.ds(start, count)], buffer.at[pl.ds(place_ * rows + start, count)],
            send_sem.at[flow, c], recv_sem.at[flow, c],
            device_id=on(block), device_id_type=MESH,
        )

    def give_back(flow, r):
        part = pl.ds(r * back, back)
        block = (peer, lent_by, far_by)[flow]
        return pltpu.make_async_remote_copy(
            give.at[flow, part], got.at[flow, part],
            back_send_sem.at[flow, r], back_recv_sem.at[flow, r],
            device_id=on(block), device_id_type=MESH,
        )

    def begin(ready, flow, c):
        if flow == 2:
            ready = jnp.logical_and(ready, odd == 1)
        pl.when(ready)(lambda: send(flow, c).start())

    def begin(ready, flow, c):
        if flow == 2:
            ready = jnp.logical_and(ready, odd == 1)
        pl.when(ready)(lambda: send(flow, c).start())

    for c, (start, count) in enumerate(CUTS):
        load(image_ref, core, c).wait()
        load(text_ref, 1 - core, c).wait()

        def normalize(k, _):
            part = pl.ds(pl.multiple_of(start + k * 64, 64), 64)
            for slot, buffer in enumerate((firsts, seconds)):
                values = raw[slot, part].astype(jnp.float32)
                inverse = lax.rsqrt(jnp.sum(values * values, axis=1, keepdims=True) + epsilon)
                inv[slot, part] = inverse
                buffer[part] = (values * inverse).astype(jnp.bfloat16)
            return 0

        lax.fori_loop(0, count // 64, normalize, 0)
        if c == 0:
            pl.semaphore_wait(barrier, 3 + 2 * odd)
        for half, plan in enumerate((LOWER, UPPER)):
            for flow, piece in plan[0]:
                if piece == c:
                    begin(upper == half, flow, piece)

    def gate(half, c):
        here = upper == half
        pl.when(here)(lambda: send(half, c).wait_send())
        for flow, piece in (LOWER, UPPER)[half][1 + c]:
            begin(here, flow, piece)

    temper = scale_ref[0]
    offset = bias_ref[0]

    def weigh(first, last, start, count, own=False):
        def step(k, _):
            part = pl.ds(pl.multiple_of(k * STEP, STEP), STEP)
            logits = lax.dot_general(
                firsts[part], seconds[pl.ds(start, count)], (((1,), (1,)), ((), ())),
                preferred_element_type=jnp.float32,
            )
            slope = jax.nn.sigmoid(temper * logits + offset)
            if own:
                row = lax.broadcasted_iota(jnp.int32, logits.shape, 0) + k * STEP
                column = lax.broadcasted_iota(jnp.int32, logits.shape, 1)
                slope = slope - jnp.where(row == column, 1.0, 0.0)
            weights[part, pl.ds(start, count)] = (temper * slope).astype(jnp.bfloat16)
            return 0

        lax.fori_loop(first, last, step, 0)

    def first_sum(base, k, start, count):
        part = pl.ds(pl.multiple_of(base + k * STEP, STEP), STEP)
        across = pl.ds(start, count)
        return jnp.dot(weights[part, across], seconds[across], preferred_element_type=jnp.float32)

    def second_sum(base, k, start, count):
        part = pl.ds(pl.multiple_of(base + k * STEP, STEP), STEP)
        down = pl.ds(start, count)
        return lax.dot_general(
            weights[down, part], firsts[down], (((0,), (0,)), ((), ())),
            preferred_element_type=jnp.float32,
        )

    def flush(flow, k):
        if flow == 0:
            first_at = pl.multiple_of(odd * rows, rows)
            total = first_sum(rows, k, first_at, 2 * rows)
        elif flow == 1:
            total = second_sum(rows, k, 0, 2 * rows)
        else:
            total = second_sum(2 * rows, k, rows, rows)
        give[flow, pl.ds(pl.multiple_of(k * STEP, STEP), STEP)] = total.astype(jnp.bfloat16)
        for h in range(STEP // back):
            give_back(flow, k * (STEP // back) + h).start()

    blocks = rows // STEP
    whole = CUTS[0][1] // STEP
    weigh(0, blocks, 0, rows, own=True)
    gate(0, 0)
    gate(1, 0)
    gate(1, 1)
    send(1, 0).wait_recv()
    weigh(0, blocks, rows, CUTS[0][1])
    gate(0, 1)
    send(0, 0).wait_recv()
    weigh(blocks, blocks + whole, rows, CUTS[0][1])
    pl.when(odd == 0)(lambda: weigh(blocks, blocks + whole, 0, rows))
    send(0, 1).wait_recv()
    weigh(blocks + whole, 2 * blocks, rows, CUTS[0][1])
    pl.when(odd == 0)(lambda: weigh(blocks + whole, 2 * blocks, 0, rows))
    flush(1, 0)
    send(1, 1).wait_recv()
    weigh(blocks, 2 * blocks, rows + CUTS[1][0], CUTS[1][1])
    pl.when(odd == 0)(lambda: flush(0, 0))
    flush(1, 1)
    pl.when(odd == 0)(lambda: flush(0, 1))
    weigh(0, blocks, rows + CUTS[1][0], CUTS[1][1])
    flush(1, 2)
    pl.when(odd == 0)(lambda: flush(0, 2))

    @pl.when(odd == 1)
    def _():
        for c in range(PARTS):
            send(2, c).wait_recv()
        weigh(blocks, 2 * blocks, 2 * rows, rows)

        def both(k, _):
            flush(0, k)
            flush(2, k)
            return 0

        lax.fori_loop(0, blocks, both, 0)

    def own_sums(k, _):
        part = pl.ds(pl.multiple_of(k * STEP, STEP), STEP)
        out[0, part] = first_sum(0, k, 0, 2 * rows)

        @pl.when(odd == 0)
        def _():
            out[1, part] = second_sum(0, k, 0, 2 * rows)

        @pl.when(odd == 1)
        def _():
            out[1, part] = second_sum(0, k, 0, rows)

        return 0

    lax.fori_loop(0, blocks, own_sums, 0)

    def finish(r, _):
        part = pl.ds(pl.multiple_of(r * back, back), back)
        give_back(0, r).wait_recv()
        give_back(1, r).wait_recv()
        out[0, part] += got[0, part].astype(jnp.float32)
        out[1, part] += got[1, part].astype(jnp.float32)

        @pl.when(odd == 1)
        def _():
            give_back(2, r).wait_recv()
            out[1, part] += got[2, part].astype(jnp.float32)

        for slot in (0, 1):
            inverse = inv[slot, part]
            unit = raw[slot, part].astype(jnp.float32) * inverse
            grad = out[slot, part]
            out[slot, part] = (
                grad - unit * jnp.sum(unit * grad, axis=1, keepdims=True)
            ) * inverse
        return 0

    lax.fori_loop(0, BACK, finish, 0)

    for c in range(PARTS):
        pl.when(upper == 0)(lambda c=c: send(1, c).wait_send())
        pl.when(upper == 1)(lambda c=c: send(0, c).wait_send())
        pl.when(odd == 1)(lambda c=c: send(2, c).wait_send())
    for r in range(BACK):
        give_back(0, r).wait_send()
        give_back(1, r).wait_send()
        pl.when(odd == 1)(lambda r=r: give_back(2, r).wait_send())


def write_out(sums, image_out, text_out, sem):
    core = lax.rem(lax.axis_index("dp"), 2)
    copies = [
        pltpu.make_async_copy(sums.at[core], image_out, sem.at[0]),
        pltpu.make_async_copy(sums.at[1 - core], text_out, sem.at[1]),
    ]
    for copy in copies:
        copy.start()
    for copy in copies:
        copy.wait()


def shards(image_embed, text_embed, logit_scale, logit_bias):
    rows, width = image_embed.shape
    stack = lambda n, kind: pltpu.VMEM((n, rows, width), kind)
    result = jax.ShapeDtypeStruct((rows, width), jnp.float32)
    sums = pl.pallas_call(
        kernel,
        out_shape=pltpu.VMEM((2, rows, width), jnp.float32),
        in_specs=[pl.BlockSpec(memory_space=pl.ANY)] * 2
        + [pl.BlockSpec(memory_space=pltpu.SMEM)] * 2,
        out_specs=pl.BlockSpec(memory_space=pltpu.VMEM),
        scratch_shapes=[
            stack(2, jnp.bfloat16),
            pltpu.VMEM((2, rows, 1), jnp.float32),
            pltpu.VMEM((2 * rows, width), jnp.bfloat16),
            pltpu.VMEM((3 * rows, width), jnp.bfloat16),
            pltpu.VMEM((2 * rows, 3 * rows), jnp.bfloat16),
            stack(3, jnp.bfloat16),
            stack(3, jnp.bfloat16),
            pltpu.SemaphoreType.DMA((2, PARTS)),
            pltpu.SemaphoreType.DMA((3, PARTS)),
            pltpu.SemaphoreType.DMA((3, PARTS)),
            pltpu.SemaphoreType.DMA((3, BACK)),
            pltpu.SemaphoreType.DMA((3, BACK)),
        ],
        compiler_params=pltpu.CompilerParams(
            collective_id=0, has_side_effects=True, vmem_limit_bytes=50 * 1024 * 1024
        ),
        cost_estimate=pl.CostEstimate(
            flops=24 * rows * rows * width, bytes_accessed=12 * rows * width,
            transcendentals=4 * rows * rows,
        ),
        name="pair_gradients",
    )(image_embed, text_embed, logit_scale, logit_bias)
    return tuple(
        pl.pallas_call(
            write_out,
            out_shape=[result] * 2,
            in_specs=[pl.BlockSpec(memory_space=pltpu.VMEM)],
            out_specs=[pl.BlockSpec(memory_space=pl.ANY)] * 2,
            scratch_shapes=[pltpu.SemaphoreType.DMA((2,))],
            cost_estimate=pl.CostEstimate(
                flops=0, bytes_accessed=16 * rows * width, transcendentals=0
            ),
            compiler_params=pltpu.CompilerParams(vmem_limit_bytes=8 * 1024 * 1024),
            name="write_out",
        )(pltpu.with_memory_space_constraint(sums, pltpu.VMEM))
    )


def solution(mesh):
    return jax.shard_map(
        shards,
        mesh=mesh,
        in_specs=(P(("dp", "blk"), None), P(("dp", "blk"), None), P(), P()),
        out_specs=(P(("dp", "blk"), None), P(("dp", "blk"), None)),
        check_vma=False,
    )
```

time: 107 us -> 100 us (0.935)
  local copies, waits for them, and re-layouts: 5.97 us -> 0 us
    unnamed x4 -> x0, local copies, waits for them, and re-layouts: 5.97 us -> none
    pallas_call x1 -> x2, Pallas kernels: 98.6 us -> 97.9 us  [the longest x1 94.9 us: shards(): pl.pallas_call(kernel, out_shape=pltpu.VMEM((2, rows, width), jnp.float32...]
where the time goes in v2:
time: 100 us
  Pallas kernels  97.9 us (98%)
  between operations  2.09 us (2%)
    pallas_call x1, Pallas kernels, shards(): pl.pallas_call(kernel, out_shape=pltpu.VMEM((2, rows, width), jnp.float32...  94.9 us
    pallas_call x1, Pallas kernels, shards(): pl.pallas_call(write_out, out_shape=[result] * 2, in_specs=[pl.BlockSpec(...  2.99 us

profile of v2, /device:TPU:1, one launch (start us, length us, event | category | flops | bytes accessed | tf_op | source)
XLA Modules:
  0.0 100.0 jit_solution(17459150147070314414)
XLA Ops:
  1.9 94.9 %pair_gradients.1.sums = f32[2,768,1152]{2,1,0:T(8,128)S(1)} custom-call(bf16[768,1152]{1,0:T(8,128)(2,1)} %image_ref.1, bf16[768,1152]{1,0:T(8,128)(2,1)} %text_ref.1, f32[1]{0:T(128)S(6)} %copy.6.scale_ref, f32[1]{0:T(128)S(6)} %copy.7.bias_ref), custom_call_target="tpu_custom_call" | custom-call | flops 16307453952 | bytes 10616832 | tf_op jit(solution)/shard_map/pair_gradients/pallas_call | solution.py:276
  96.9 3.0 %write_out.1 = (f32[768,1152]{1,0:T(8,128)}, f32[768,1152]{1,0:T(8,128)}) custom-call(f32[2,768,1152]{2,1,0:T(8,128)S(1)} %pair_gradients.1.sums), custom_call_target="tpu_custom_call" | custom-call | bytes 14155776 | tf_op jit(solution)/shard_map/write_out/pallas_call | solution.py:306

commit v3 on v2

--- a/solution.py
+++ b/solution.py
@@ -9,15 +9,17 @@
 
 MESH = pl.DeviceIdType.MESH
 ROW = 4
-CUTS = ((0, 512), (512, 256))
-PARTS = len(CUTS)
-STEP = 256
+PARTS = 3
 BACK = 6
 
 epsilon = 1e-06
 
-LOWER = ([(0, 0), (2, 0), (0, 1)], [(1, 0), (2, 1)], [(1, 1)])
-UPPER = ([(1, 0), (1, 1)], [(0, 0), (2, 0)], [(0, 1), (2, 1)])
+LOWER = (
+    [(0, 0), (0, 1), (0, 2)], [], [(2, 0)], [(1, 0), (1, 1), (2, 1), (1, 2), (2, 2)],
+)
+UPPER = (
+    [(1, 0), (1, 1), (1, 2)], [], [], [(0, 0), (2, 0), (0, 1), (2, 1), (0, 2), (2, 2)],
+)
 
 
 def kernel(
@@ -27,6 +29,7 @@
 ):
     rows, _ = image_ref.shape
     back = rows // BACK
+    size = rows // PARTS
     blk = lax.axis_index("blk")
     core = lax.rem(lax.axis_index("dp"), 2)
     x = lax.rem(blk, ROW)
@@ -59,7 +62,7 @@
             pl.semaphore_signal(barrier, inc=1, device_id=on(block), device_id_type=MESH)
 
     def load(source, slot, c):
-        part = pl.ds(*CUTS[c])
+        part = pl.ds(c * size, size)
         return pltpu.make_async_copy(
             source.at[part], raw.at[slot, part], load_sem.at[slot, c]
         )
@@ -69,7 +72,7 @@
         load(text_ref, 1 - core, c).start()
 
     def send(flow, c):
-        start, count = CUTS[c]
+        start, count = c * size, size
         buffer, place_, block = (
             (firsts, 1, peer), (seconds, 1, lent_to), (seconds, 2, far_to)
         )[flow]
@@ -98,7 +101,8 @@
             ready = jnp.logical_and(ready, odd == 1)
         pl.when(ready)(lambda: send(flow, c).start())
 
-    for c, (start, count) in enumerate(CUTS):
+    for c in range(PARTS):
+        start, count = c * size, size
         load(image_ref, core, c).wait()
         load(text_ref, 1 - core, c).wait()
 
@@ -130,14 +134,14 @@
 
     def weigh(first, last, start, count, own=False):
         def step(k, _):
-            part = pl.ds(pl.multiple_of(k * STEP, STEP), STEP)
+            part = pl.ds(pl.multiple_of(k * size, size), size)
             logits = lax.dot_general(
                 firsts[part], seconds[pl.ds(start, count)], (((1,), (1,)), ((), ())),
                 preferred_element_type=jnp.float32,
             )
             slope = jax.nn.sigmoid(temper * logits + offset)
             if own:
-                row = lax.broadcasted_iota(jnp.int32, logits.shape, 0) + k * STEP
+                row = lax.broadcasted_iota(jnp.int32, logits.shape, 0) + k * size
                 column = lax.broadcasted_iota(jnp.int32, logits.shape, 1)
                 slope = slope - jnp.where(row == column, 1.0, 0.0)
             weights[part, pl.ds(start, count)] = (temper * slope).astype(jnp.bfloat16)
@@ -146,19 +150,19 @@
         lax.fori_loop(first, last, step, 0)
 
     def first_sum(base, k, start, count):
-        part = pl.ds(pl.multiple_of(base + k * STEP, STEP), STEP)
+        part = pl.ds(pl.multiple_of(base + k * size, size), size)
         across = pl.ds(start, count)
         return jnp.dot(weights[part, across], seconds[across], preferred_element_type=jnp.float32)
 
     def second_sum(base, k, start, count):
-        part = pl.ds(pl.multiple_of(base + k * STEP, STEP), STEP)
+        part = pl.ds(pl.multiple_of(base + k * size, size), size)
         down = pl.ds(start, count)
         return lax.dot_general(
             weights[down, part], firsts[down], (((0,), (0,)), ((), ())),
             preferred_element_type=jnp.float32,
         )
 
-    def flush(flow, k):
+    def form(flow, k):
         if flow == 0:
             first_at = pl.multiple_of(odd * rows, rows)
             total = first_sum(rows, k, first_at, 2 * rows)
@@ -166,50 +170,75 @@
             total = second_sum(rows, k, 0, 2 * rows)
         else:
             total = second_sum(2 * rows, k, rows, rows)
-        give[flow, pl.ds(pl.multiple_of(k * STEP, STEP), STEP)] = total.astype(jnp.bfloat16)
-        for h in range(STEP // back):
-            give_back(flow, k * (STEP // back) + h).start()
-
-    blocks = rows // STEP
-    whole = CUTS[0][1] // STEP
-    weigh(0, blocks, 0, rows, own=True)
-    gate(0, 0)
-    gate(1, 0)
-    gate(1, 1)
-    send(1, 0).wait_recv()
-    weigh(0, blocks, rows, CUTS[0][1])
-    gate(0, 1)
-    send(0, 0).wait_recv()
-    weigh(blocks, blocks + whole, rows, CUTS[0][1])
-    pl.when(odd == 0)(lambda: weigh(blocks, blocks + whole, 0, rows))
-    send(0, 1).wait_recv()
-    weigh(blocks + whole, 2 * blocks, rows, CUTS[0][1])
-    pl.when(odd == 0)(lambda: weigh(blocks + whole, 2 * blocks, 0, rows))
-    flush(1, 0)
-    send(1, 1).wait_recv()
-    weigh(blocks, 2 * blocks, rows + CUTS[1][0], CUTS[1][1])
-    pl.when(odd == 0)(lambda: flush(0, 0))
-    flush(1, 1)
-    pl.when(odd == 0)(lambda: flush(0, 1))
-    weigh(0, blocks, rows + CUTS[1][0], CUTS[1][1])
-    flush(1, 2)
-    pl.when(odd == 0)(lambda: flush(0, 2))
+        give[flow, pl.ds(pl.multiple_of(k * size, size), size)] = total.astype(jnp.bfloat16)
+
+    def launch(flow, k):
+        for h in range(BACK // PARTS):
+            give_back(flow, k * (BACK // PARTS) + h).start()
+
+    def early(flow, k):
+        form(flow, k)
+        pl.when(upper == 1)(lambda: launch(flow, k))
+
+    def if_even(action):
+        pl.when(odd == 0)(action)
+
+    weigh(0, PARTS, 0, rows, own=True)
+    for c in range(PARTS):
+        gate(0, c)
+        gate(1, c)
+    last = PARTS - 1
+    for c in range(last):
+        send(1, c).wait_recv()
+        weigh(0, PARTS, rows + c * size, size)
+        send(0, c).wait_recv()
+        if_even(lambda: weigh(PARTS + c, PARTS + c + 1, 0, rows))
+        weigh(PARTS + c, PARTS + c + 1, rows, (c + 1) * size)
+        if c > 0:
+            weigh(PARTS, PARTS + c, rows + c * size, size)
+    send(1, last).wait_recv()
+    weigh(PARTS, PARTS + last, rows + last * size, size)
+    if_even(lambda: early(0, 0))
+    send(0, last).wait_recv()
+    weigh(PARTS + last, PARTS + last + 1, rows, rows)
+    early(1, 0)
+    if_even(lambda: early(0, 1))
+    early(1, 1)
+    if_even(lambda: weigh(PARTS + last, PARTS + last + 1, 0, rows))
+    if_even(lambda: early(0, last))
+    weigh(0, PARTS, rows + last * size, size)
+    early(1, last)
+
+    def weigh_far(c):
+        send(2, c).wait_recv()
+        weigh(PARTS, 2 * PARTS, 2 * rows + c * size, size)
 
     @pl.when(odd == 1)
     def _():
-        for c in range(PARTS):
-            send(2, c).wait_recv()
-        weigh(blocks, 2 * blocks, 2 * rows, rows)
+        for c in range(last):
+            weigh_far(c)
+
+    @pl.when(upper == 0)
+    def _():
+        for k in range(PARTS):
+            launch(1, k)
+            if_even(lambda k=k: launch(0, k))
+
+    @pl.when(odd == 1)
+    def _():
+        weigh_far(last)
 
         def both(k, _):
-            flush(0, k)
-            flush(2, k)
+            form(0, k)
+            launch(0, k)
+            form(2, k)
+            launch(2, k)
             return 0
 
-        lax.fori_loop(0, blocks, both, 0)
+        lax.fori_loop(0, PARTS, both, 0)
 
     def own_sums(k, _):
-        part = pl.ds(pl.multiple_of(k * STEP, STEP), STEP)
+        part = pl.ds(pl.multiple_of(k * size, size), size)
         out[0, part] = first_sum(0, k, 0, 2 * rows)
 
         @pl.when(odd == 0)
@@ -222,7 +251,7 @@
 
         return 0
 
-    lax.fori_loop(0, blocks, own_sums, 0)
+    lax.fori_loop(0, PARTS, own_sums, 0)
 
     def finish(r, _):
         part = pl.ds(pl.multiple_of(r * back, back), back)
@@ -248,8 +277,8 @@
     lax.fori_loop(0, BACK, finish, 0)
 
     for c in range(PARTS):
+        pl.when(upper == 1)(lambda c=c: send(0, c).wait_send())
         pl.when(upper == 0)(lambda c=c: send(1, c).wait_send())
-        pl.when(upper == 1)(lambda c=c: send(0, c).wait_send())
         pl.when(odd == 1)(lambda c=c: send(2, c).wait_send())
     for r in range(BACK):
         give_back(0, r).wait_send()

time: 100 us -> 98.8 us (0.988); the launches traced: 100 us -> 97.6 us
  Pallas kernels: 97.9 us -> 95.5 us
    pallas_call x1, Pallas kernels: 94.9 us -> 92.5 us  [shards(): pl.pallas_call(kernel, out_shape=pltpu.VMEM((2, rows, width), jnp.float32...]
where the time goes in v3:
time: 98.8 us; the launch traced here: 97.6 us
  Pallas kernels  95.5 us (97%)
  between operations  2.09 us (2%)
    pallas_call x1, Pallas kernels, shards(): pl.pallas_call(kernel, out_shape=pltpu.VMEM((2, rows, width), jnp.float32...  92.5 us
    pallas_call x1, Pallas kernels, shards(): pl.pallas_call(write_out, out_shape=[result] * 2, in_specs=[pl.BlockSpec(...  2.99 us

profile of v3, /device:TPU:1, one launch (start us, length us, event | category | flops | bytes accessed | tf_op | source)
XLA Modules:
  0.0 97.6 jit_solution(5191617351204583173)
XLA Ops:
  1.9 92.5 %pair_gradients.1.sums = f32[2,768,1152]{2,1,0:T(8,128)S(1)} custom-call(bf16[768,1152]{1,0:T(8,128)(2,1)} %image_ref.1, bf16[768,1152]{1,0:T(8,128)(2,1)} %text_ref.1, f32[1]{0:T(128)S(6)} %copy.6.scale_ref, f32[1]{0:T(128)S(6)} %copy.7.bias_ref), custom_call_target="tpu_custom_call" | custom-call | flops 16307453952 | bytes 10616832 | tf_op jit(solution)/shard_map/pair_gradients/pallas_call | solution.py:305
  94.5 3.0 %write_out.1 = (f32[768,1152]{1,0:T(8,128)}, f32[768,1152]{1,0:T(8,128)}) custom-call(f32[2,768,1152]{2,1,0:T(8,128)S(1)} %pair_gradients.1.sums), custom_call_target="tpu_custom_call" | custom-call | bytes 14155776 | tf_op jit(solution)/shard_map/write_out/pallas_call | solution.py:335

commit v4 on v3

--- a/solution.py
+++ b/solution.py
@@ -229,10 +229,10 @@
         weigh_far(last)
 
         def both(k, _):
+            form(2, k)
+            launch(2, k)
             form(0, k)
             launch(0, k)
-            form(2, k)
-            launch(2, k)
             return 0
 
         lax.fori_loop(0, PARTS, both, 0)

time: 98.8 us -> 98.5 us (level)
  no operation moved by 1% of the time
where the time goes in v4:
time: 98.5 us; the launch traced here: 97 us
  Pallas kernels  94.9 us (96%)
  between operations  2.09 us (2%)
    pallas_call x1, Pallas kernels, shards(): pl.pallas_call(kernel, out_shape=pltpu.VMEM((2, rows, width), jnp.float32...  91.9 us
    pallas_call x1, Pallas kernels, shards(): pl.pallas_call(write_out, out_shape=[result] * 2, in_specs=[pl.BlockSpec(...  2.99 us

profile of v4, /device:TPU:1, one launch (start us, length us, event | category | flops | bytes accessed | tf_op | source)
XLA Modules:
  0.0 97.0 jit_solution(16676274244401792490)
XLA Ops:
  1.9 91.9 %pair_gradients.1.sums = f32[2,768,1152]{2,1,0:T(8,128)S(1)} custom-call(bf16[768,1152]{1,0:T(8,128)(2,1)} %image_ref.1, bf16[768,1152]{1,0:T(8,128)(2,1)} %text_ref.1, f32[1]{0:T(128)S(6)} %copy.6.scale_ref, f32[1]{0:T(128)S(6)} %copy.7.bias_ref), custom_call_target="tpu_custom_call" | custom-call | flops 16307453952 | bytes 10616832 | tf_op jit(solution)/shard_map/pair_gradients/pallas_call | solution.py:305
  93.9 3.0 %write_out.1 = (f32[768,1152]{1,0:T(8,128)}, f32[768,1152]{1,0:T(8,128)}) custom-call(f32[2,768,1152]{2,1,0:T(8,128)S(1)} %pair_gradients.1.sums), custom_call_target="tpu_custom_call" | custom-call | bytes 14155776 | tf_op jit(solution)/shard_map/write_out/pallas_call | solution.py:335
